TPU v7x, 256 devices: a whole 4x4x8 slice. The times are simulated.
256 devices in a mesh: acct: 64 (over x, z, core), rep: 4 (over y).
Axes of the slice: x: 4, y: 4, z: 8, core: 2. Of those that a mesh axis runs over, the one named last changes fastest.
Arguments:
- right_side: float32 [1048576, 64], P(('acct', 'rep')), may hold values from -6 to 6
- tile_account: int32 [16384, 128], P(('acct', 'rep')), may hold values from 0 to 127
- tile_attribute: int32 [16384, 128], P(('acct', 'rep')), may hold values from 0 to 127
- tile_count: int32 [16384], P(('acct', 'rep')), may hold values from 1 to 128
- tile_home: int32 [16384], P(('acct', 'rep')), may hold values from 0 to 31
- tile_block: int32 [16384], P(('acct', 'rep')), may hold values from 0 to 3
- attribute_weight: int32 [32768], P('acct'), may hold values from 1 to 4
Outputs:
- solution: float32 [1048576, 64], P(('acct', 'rep'))
- residual: float32 [1048576, 64], P(('acct', 'rep'))
All inputs are finite; a program needn't handle non-finite values.
Results may differ from a plain program's by a relative error of at most 0.00035.
Values sent between devices are 32-bit elements; how exact they have to be, the bound alone decides.
No kernel may reach another device: no remote copies, remote signals or barrier semaphores. Data moves between devices by JAX's collectives and lax.ppermute only.
A program may use at most 64 MiB of HBM per device.

v0:
```python
import jax
import jax.numpy as jnp
from jax import lax
from jax.sharding import PartitionSpec as P

ITERS = 3


def solve_spd(matrix, target):
    factor = jnp.linalg.cholesky(matrix)
    partway = lax.linalg.triangular_solve(factor, target, left_side=True, lower=True)
    return lax.linalg.triangular_solve(
        factor, partway, left_side=True, lower=True, transpose_a=True
    )


def inner_gram(first, second):
    return jnp.dot(first.T, second, precision=lax.Precision.HIGHEST)


def dense_tiles(account_list, attrib_list, counts, slot_ids):
    usable = (slot_ids[None, :] < counts[:, None]).astype(jnp.float32)
    account_hot = (account_list[:, :, None] == slot_ids).astype(jnp.float32) * usable[:, :, None]
    attrib_hot = (attrib_list[:, :, None] == slot_ids).astype(jnp.float32)
    return jnp.einsum("tsa,tsb->tab", account_hot, attrib_hot, precision=lax.Precision.HIGHEST)


def shards(
    right_side, tile_account, tile_attribute, tile_count, tile_home, tile_block, attribute_weight
):
    tile_total, tile_width = tile_account.shape
    account_rows, columns = right_side.shape
    home_blocks = account_rows // tile_width
    attr_blocks = attribute_weight.shape[0] // tile_width
    exact_result = lax.Precision.HIGHEST
    slot_ids = jnp.arange(tile_width, dtype=jnp.int32)
    local_tile_set = dense_tiles(tile_account, tile_attribute, tile_count, slot_ids)
    home_onehot_matrix = (tile_home[:, None] == jnp.arange(home_blocks, dtype=jnp.int32)).astype(
        jnp.float32
    )
    block_hot = (tile_block[:, None] == jnp.arange(attr_blocks, dtype=jnp.int32)).astype(
        jnp.float32
    )
    weight = attribute_weight.astype(jnp.float32).reshape(attr_blocks, tile_width)
    column_counts = jnp.sum(local_tile_set, axis=1)
    counts_in, block_in = (
        lax.all_to_all(column_counts, "acct", split_axis=0, concat_axis=0, tiled=True),
        lax.all_to_all(block_hot, "acct", split_axis=0, concat_axis=0, tiled=True),
    )
    attr_counts = jnp.einsum("tk,ta->ka", block_in, counts_in, precision=exact_result)
    attr_counts = lax.psum(attr_counts, "rep")
    weighted = attr_counts * weight
    back_counts = jnp.einsum("tk,ka->ta", block_in, weighted, precision=exact_result)
    own_values = lax.all_to_all(back_counts, "acct", split_axis=0, concat_axis=0, tiled=True)
    tile_degree = jnp.einsum("tab,tb->ta", local_tile_set, own_values, precision=exact_result)
    degree = jnp.einsum(
        "tk,ta->ka", home_onehot_matrix, tile_degree, precision=exact_result
    ).reshape(account_rows)
    solution = jnp.zeros((account_rows, columns), jnp.float32)
    residual = right_side
    direction = right_side
    res_gram = lax.psum(inner_gram(residual, residual), ("acct", "rep"))
    for iteration in range(ITERS):
        blocks = direction.reshape(home_blocks, tile_width, columns)
        selected_rows = jnp.take(blocks, tile_home, axis=0)
        partial_value_sum = jnp.einsum(
            "phr,phd->prd", local_tile_set, selected_rows, precision=exact_result
        )
        partial_in = lax.all_to_all(
            partial_value_sum, "acct", split_axis=0, concat_axis=0, tiled=True
        )
        summed = jnp.einsum("tk,tbc->kbc", block_in, partial_in, precision=exact_result)
        summed = lax.psum(summed, "rep")
        scaled = summed * weight[:, :, None]
        spread = jnp.einsum("tk,kbc->tbc", block_in, scaled, precision=exact_result)
        value_entries = lax.all_to_all(spread, "acct", split_axis=0, concat_axis=0, tiled=True)
        gathered_values = jnp.einsum(
            "dsu,duw->dsw", local_tile_set, value_entries, precision=exact_result
        )
        linked_entries = jnp.einsum(
            "iz,ieb->zeb", home_onehot_matrix, gathered_values, precision=exact_result
        ).reshape(account_rows, columns)
        product = direction + 0.0625 * (degree[:, None] * direction - linked_entries)
        curvature = lax.psum(inner_gram(direction, product), ("acct", "rep"))
        step_size = solve_spd(curvature, res_gram)
        solution = solution + jnp.dot(direction, step_size, precision=exact_result)
        residual = residual - jnp.dot(product, step_size, precision=exact_result)
        if iteration + 1 < ITERS:
            new_gram = lax.psum(inner_gram(residual, residual), ("acct", "rep"))
            update = solve_spd(res_gram, new_gram)
            direction = residual + jnp.dot(direction, update, precision=exact_result)
            res_gram = new_gram
    return (solution, residual)


def solution(mesh):
    return jax.shard_map(
        shards,
        mesh=mesh,
        in_specs=(
            P(("acct", "rep"), None),
            P(("acct", "rep"), None),
            P(("acct", "rep"), None),
            P(("acct", "rep")),
            P(("acct", "rep")),
            P(("acct", "rep")),
            P("acct"),
        ),
        out_specs=(P(("acct", "rep"), None), P(("acct", "rep"), None)),
        check_vma=False,
    )
```

profile of v0, /device:TPU:26, one launch (start us, length us, event | category | flops | bytes accessed | tf_op | source)
XLA Modules:
  0.0 1065.8 jit_solution(11035413211626079029)
XLA Ops:
  8.6 12.0 %all-to-all-start = ((f32[64,1,4]{2,1,0:T(1,128)}), f32[64,1,4]{2,1,0:T(1,128)S(1)}, u32[]{:S(2)}, u32[]{:S(2)}) async-start(f32[64,1,4]{2,1,0:T(1,128)} %compare_convert_fusion), calls=%async_computation | async-start | bytes 65536 | tf_op jit(solution)/shard_map/all_to_all | solution.py:48
  30.0 10.3 all-to-all-start.1
  40.4 6.7 fusion.19
  48.9 8.6 all-to-all-start.3
  57.8 7.5 psum.70
  65.3 41.8 %all-to-all-done.3 = f32[64,128,64]{1,2,0:T(8,128)S(1)} async-done(((f32[64,128,64]{1,2,0:T(8,128)}), f32[64,128,64]{1,2,0:T(8,128)S(1)}, u32[]{:S(2)}, u32[]{:S(2)}) %all-to-all-start.3) | async-done | bytes 2097184 | tf_op jit(solution)/shard_map/all_to_all | solution.py:69
  110.7 7.8 all-to-all-start.2
  118.6 34.9 %all-reduce.5.cloned.1.call-done = f32[4,128,64]{1,0,2:T(4,128)} async-done(((f32[4,128,64]{1,0,2:T(4,128)}), f32[4,128,64]{1,0,2:T(4,128)}) %all-reduce.5.cloned.1.call-update) | async-done | bytes 131088 | tf_op jit(solution)/shard_map/psum | solution.py:73
  158.7 10.7 %all-to-all-start.4 = ((f32[64,128,64]{1,2,0:T(8,128)}), f32[64,128,64]{1,2,0:T(8,128)S(1)}, u32[]{:S(2)}, u32[]{:S(2)}) async-start(f32[64,128,64]{1,2,0:T(8,128)} %copy.54), calls=%async_computation.4 | async-start | bytes 4194304 | tf_op jit(solution)/shard_map/all_to_all | solution.py:76
  170.4 8.3 fusion.71
  178.8 40.1 %all-to-all-done.4 = f32[64,128,64]{1,2,0:T(8,128)S(1)} async-done(((f32[64,128,64]{1,2,0:T(8,128)}), f32[64,128,64]{1,2,0:T(8,128)S(1)}, u32[]{:S(2)}, u32[]{:S(2)}) %all-to-all-start.4) | async-done | bytes 2097184 | tf_op jit(solution)/shard_map/all_to_all | solution.py:76
  218.9 9.9 fusion.121
  232.4 75.7 %all-reduce = (f32[64,64]{0,1:T(8,128)S(1)}, f32[64,64]{0,1:T(8,128)S(1)}) all-reduce(f32[64,64]{0,1:T(8,128)S(1)} %fusion.122, f32[64,64]{0,1:T(8,128)S(1)} %convolution_bitcast_fusion.2), channel_id=1, replica_groups=mesh['acct'=64,'rep'=4] {'acct','rep'}, use_global_device_ids=true, to_apply=%region_6.9 | all-reduce | flops 8192 | bytes 65536 | tf_op jit(solution)/shard_map/psum | solution.py:62
  323.6 73.8 %psum.74 = f32[64,64]{0,1:T(8,128)S(1)} all-reduce(f32[64,64]{0,1:T(8,128)S(1)} %fusion.123), channel_id=1, replica_groups=mesh['acct'=64,'rep'=4] {'acct','rep'}, use_global_device_ids=true, to_apply=%region_7.12 | all-reduce | flops 4096 | bytes 32768 | tf_op jit(solution)/shard_map/psum | solution.py:89
  415.2 6.0 fusion.17
  421.2 56.3 %all_to_all.63 = f32[64,128,64]{1,2,0:T(8,128)S(1)} all-to-all(f32[64,128,64]{1,2,0:T(8,128)S(1)} %fusion.17), channel_id=1, replica_groups=mesh['acct'=64,'rep'=4] {'acct'}, dimensions={0} | all-to-all | bytes 4194304 | tf_op jit(solution)/shard_map/all_to_all | solution.py:69
  480.4 43.3 %all-reduce.7.cloned.1.call-done = f32[4,128,64]{1,0,2:T(4,128)} async-done(((f32[4,128,64]{1,0,2:T(4,128)}), f32[4,128,64]{1,0,2:T(4,128)}) %all-reduce.7.cloned.1.call-update) | async-done | bytes 131088 | tf_op jit(solution)/shard_map/psum | solution.py:73
  528.9 10.7 %all-to-all-start.6 = ((f32[64,128,64]{1,2,0:T(8,128)}), f32[64,128,64]{1,2,0:T(8,128)}, u32[]{:S(2)}, u32[]{:S(2)}) async-start(f32[64,128,64]{1,2,0:T(8,128)} %copy.62), calls=%async_computation.6 | async-start | bytes 4194304 | tf_op jit(solution)/shard_map/all_to_all | solution.py:76
  540.0 5.8 cholesky.122
  552.1 37.1 %all-to-all-done.6 = f32[64,128,64]{1,2,0:T(8,128)} async-done(((f32[64,128,64]{1,2,0:T(8,128)}), f32[64,128,64]{1,2,0:T(8,128)}, u32[]{:S(2)}, u32[]{:S(2)}) %all-to-all-start.6) | async-done | bytes 2097184 | tf_op jit(solution)/shard_map/all_to_all | solution.py:76
  589.1 10.1 fusion.124
  603.8 75.5 %psum.76 = f32[64,64]{0,1:T(8,128)S(1)} all-reduce(f32[64,64]{0,1:T(8,128)S(1)} %fusion.40), channel_id=1, replica_groups=mesh['acct'=64,'rep'=4] {'acct','rep'}, use_global_device_ids=true, to_apply=%region_9.14 | all-reduce | flops 4096 | bytes 32768 | tf_op jit(solution)/shard_map/psum | solution.py:84
  679.4 5.8 cholesky.111
  696.9 73.8 %psum.77 = f32[64,64]{1,0:T(8,128)S(1)} all-reduce(f32[64,64]{1,0:T(8,128)S(1)} %fusion.125), channel_id=1, replica_groups=mesh['acct'=64,'rep'=4] {'acct','rep'}, use_global_device_ids=true, to_apply=%region_10.15 | all-reduce | flops 4096 | bytes 32768 | tf_op jit(solution)/shard_map/psum | solution.py:89
  777.7 6.0 fusion.15
  783.7 56.4 %all_to_all.64 = f32[64,128,64]{1,2,0:T(8,128)S(1)} all-to-all(f32[64,128,64]{1,2,0:T(8,128)S(1)} %fusion.15), channel_id=1, replica_groups=mesh['acct'=64,'rep'=4] {'acct'}, dimensions={0} | all-to-all | bytes 4194304 | tf_op jit(solution)/shard_map/all_to_all | solution.py:69
  843.1 43.3 %all-reduce.9.cloned.1.call-done = f32[4,128,64]{1,0,2:T(4,128)} async-done(((f32[4,128,64]{1,0,2:T(4,128)}), f32[4,128,64]{1,0,2:T(4,128)}) %all-reduce.9.cloned.1.call-update) | async-done | bytes 131088 | tf_op jit(solution)/shard_map/psum | solution.py:73
  891.6 11.4 %all-to-all-start.8 = ((f32[64,128,64]{1,2,0:T(8,128)}), f32[64,128,64]{1,2,0:T(8,128)}, u32[]{:S(2)}, u32[]{:S(2)}) async-start(f32[64,128,64]{1,2,0:T(8,128)} %copy.69), calls=%async_computation.8 | async-start | bytes 4194304 | tf_op jit(solution)/shard_map/all_to_all | solution.py:76
  906.1 46.1 %all-to-all-done.8 = f32[64,128,64]{1,2,0:T(8,128)} async-done(((f32[64,128,64]{1,2,0:T(8,128)}), f32[64,128,64]{1,2,0:T(8,128)}, u32[]{:S(2)}, u32[]{:S(2)}) %all-to-all-start.8) | async-done | bytes 2097184 | tf_op jit(solution)/shard_map/all_to_all | solution.py:76
  952.2 10.1 fusion.126
  966.0 75.5 %psum.79 = f32[64,64]{0,1:T(8,128)S(1)} all-reduce(f32[64,64]{0,1:T(8,128)S(1)} %fusion.43), channel_id=1, replica_groups=mesh['acct'=64,'rep'=4] {'acct','rep'}, use_global_device_ids=true, to_apply=%region_12.17 | all-reduce | flops 4096 | bytes 32768 | tf_op jit(solution)/shard_map/psum | solution.py:84
  1041.6 5.8 cholesky.133
  (110 shorter events, 124.0 us)
Async XLA Ops:
  7.2 16.9 %copy-start.7 = (s32[64,128]{1,0:T(8,128)S(1)}, s32[64,128]{1,0:T(8,128)}, u32[]{:S(2)}) copy-start(s32[64,128]{1,0:T(8,128)} %param.16) | copy-start | bytes 98308
  7.2 16.9 %copy-start.8 = (s32[64,128]{1,0:T(8,128)S(1)}, s32[64,128]{1,0:T(8,128)}, u32[]{:S(2)}) copy-start(s32[64,128]{1,0:T(8,128)} %param.15) | copy-start | bytes 98308
  8.6 21.4 %all-to-all-start = ((f32[64,1,4]{2,1,0:T(1,128)}), f32[64,1,4]{2,1,0:T(1,128)S(1)}, u32[]{:S(2)}, u32[]{:S(2)}) async-start(f32[64,1,4]{2,1,0:T(1,128)} %compare_convert_fusion), calls=%async_computation | async-start | bytes 65536 | tf_op jit(solution)/shard_map/all_to_all | solution.py:48
  30.0 18.9 %all-to-all-start.1 = ((f32[64,1,128]{2,1,0:T(1,128)}), f32[64,1,128]{2,1,0:T(1,128)S(1)}, u32[]{:S(2)}, u32[]{:S(2)}) async-start(f32[64,1,128]{2,1,0:T(1,128)} %bitcast.1), calls=%async_computation.1 | async-start | bytes 65536 | tf_op jit(solution)/shard_map/all_to_all | solution.py:47
  47.1 10.5 copy-start.5
  48.9 58.2 %all-to-all-start.3 = ((f32[64,128,64]{1,2,0:T(8,128)}), f32[64,128,64]{1,2,0:T(8,128)S(1)}, u32[]{:S(2)}, u32[]{:S(2)}) async-start(f32[64,128,64]{1,2,0:T(8,128)} %fusion.19), calls=%async_computation.3 | async-start | bytes 4194304 | tf_op jit(solution)/shard_map/all_to_all | solution.py:69
  57.5 95.9 %all-reduce.5.cloned.1.call-start = ((), (), s32[]{:S(2)}) async-start(), calls=%async_computation.9 | async-start | bytes 262144 | tf_op jit(solution)/shard_map/psum | solution.py:73
  110.7 47.9 %all-to-all-start.2 = ((f32[64,1,128]{2,1,0:T(1,128)}), f32[64,1,128]{2,1,0:T(1,128)S(1)}, u32[]{:S(2)}, u32[]{:S(2)}) async-start(f32[64,1,128]{2,1,0:T(1,128)} %bitcast.5), calls=%async_computation.2 | async-start | bytes 65536 | tf_op jit(solution)/shard_map/all_to_all | solution.py:54
  158.7 10.7 %copy-start = (f32[4096,64]{0,1:T(8,128)S(1)}, f32[4096,64]{0,1:T(8,128)}, u32[]{:S(2)}) copy-start(f32[4096,64]{0,1:T(8,128)} %param.14) | copy-start | bytes 3145732
  158.7 60.2 %all-to-all-start.4 = ((f32[64,128,64]{1,2,0:T(8,128)}), f32[64,128,64]{1,2,0:T(8,128)S(1)}, u32[]{:S(2)}, u32[]{:S(2)}) async-start(f32[64,128,64]{1,2,0:T(8,128)} %copy.54), calls=%async_computation.4 | async-start | bytes 4194304 | tf_op jit(solution)/shard_map/all_to_all | solution.py:76
  169.3 354.4 %all-reduce.7.cloned.1.call-start = ((), (), s32[]{:S(2)}) async-start(), calls=%async_computation.10 | async-start | bytes 262144 | tf_op jit(solution)/shard_map/psum | solution.py:73
  170.4 8.3 copy-start.6
  528.9 60.2 %all-to-all-start.6 = ((f32[64,128,64]{1,2,0:T(8,128)}), f32[64,128,64]{1,2,0:T(8,128)}, u32[]{:S(2)}, u32[]{:S(2)}) async-start(f32[64,128,64]{1,2,0:T(8,128)} %copy.62), calls=%async_computation.6 | async-start | bytes 4194304 | tf_op jit(solution)/shard_map/all_to_all | solution.py:76
  539.7 346.7 %all-reduce.9.cloned.1.call-start = ((), (), s32[]{:S(2)}) async-start(), calls=%async_computation.11 | async-start | bytes 262144 | tf_op jit(solution)/shard_map/psum | solution.py:73
  601.3 1.0 copy-start.3
  695.0 1.0 copy-start.1
  891.6 60.6 %all-to-all-start.8 = ((f32[64,128,64]{1,2,0:T(8,128)}), f32[64,128,64]{1,2,0:T(8,128)}, u32[]{:S(2)}, u32[]{:S(2)}) async-start(f32[64,128,64]{1,2,0:T(8,128)} %copy.69), calls=%async_computation.8 | async-start | bytes 4194304 | tf_op jit(solution)/shard_map/all_to_all | solution.py:76
  964.4 89.8 %copy-start.2 = (f32[4096,64]{0,1:T(8,128)S(1)}, f32[4096,64]{0,1:T(8,128)}, u32[]{:S(2)}) copy-start(f32[4096,64]{0,1:T(8,128)} %copy-done.1) | copy-start | bytes 3145732
  1054.3 2.8 copy-start.4
Sparse Core Ops, SparseCore 0:
  110.1 43.3 all-reduce.4
  480.5 43.1 all-reduce.6
  843.2 43.1 all-reduce.8
where the time goes:
time: 1080 us; the launch traced here: 1070 us
  blocking collectives  495 us (46%)
  waiting for transfers between devices  288 us (27%)
  matrix products  112 us (10%)
  starting transfers between devices  71.9 us (7%)
  other arithmetic  64 us (6%)
  local copies, waits for them, and re-layouts  20.7 us (2%)
  between operations  14.5 us (1%)
    psum x2, blocking collectives, shards(): curvature = lax.psum(inner_gram(direction, product), ('acct', 'rep'))  151 us
    psum x2, blocking collectives, shards(): new_gram = lax.psum(inner_gram(residual, residual), ('acct', 'rep'))  148 us
    all_to_all x3, waiting for transfers between devices, shards(): lax.all_to_all(spread, 'acct', split_axis=0, concat_axis=0, tiled=True)  123 us
    psum x3, waiting for transfers between devices, shards(): summed = lax.psum(summed, 'rep')  122 us
    all_to_all x2, blocking collectives, shards(): lax.all_to_all(partial_value_sum, 'acct', split_axis=0, concat_axis=0, ti...  113 us
    psum x1, blocking collectives, shards(): res_gram = lax.psum(inner_gram(residual, residual), ('acct', 'rep'))  75.7 us
    all_to_all x1, waiting for transfers between devices, shards(): lax.all_to_all(partial_value_sum, 'acct', split_axis=0, concat_axis=0, ti...  41.8 us
    all_to_all x3, starting transfers between devices, shards(): lax.all_to_all(spread, 'acct', split_axis=0, concat_axis=0, tiled=True)  32.8 us
  transfers between devices with their start and end apart: 10, of which 8 were waited for; matrix products, arithmetic and copies ran while one was open for 4% of the time, Pallas kernels for 0%

commit v1 on v0

v1 whole, which is shorter than its diff:
```python
import jax
import jax.numpy as jnp
from jax import lax
from jax.experimental import pallas as pl
from jax.experimental.pallas import tpu as pltpu
from jax.sharding import Mesh, PartitionSpec as P

ITERS = 3
NX, NZ, NC, NY = 4, 8, 2, 4
TILE = 128
COLS = 64
BLOCKS = 4
HALF = NZ // 2
COUPLING = 0.0625
ALL = ("x", "z", "core", "rep")
VMEM = pl.BlockSpec(memory_space=pltpu.VMEM)
SMEM = pl.BlockSpec(memory_space=pltpu.SMEM)
NT = (((1,), (1,)), ((), ()))
PARAMS = pltpu.CompilerParams(vmem_limit_bytes=40 * 1024 * 1024)


def shape(*dims, dtype=jnp.float32):
    return jax.ShapeDtypeStruct(dims, dtype)


def solve_spd(matrix, target):
    factor = jnp.linalg.cholesky(matrix)
    partway = lax.linalg.triangular_solve(factor, target, left_side=True, lower=True)
    return lax.linalg.triangular_solve(
        factor, partway, left_side=True, lower=True, transpose_a=True
    )


def mul(first, second):
    return jnp.dot(first, second, precision=lax.Precision.HIGHEST)


def gram(first, second):
    return lax.dot_general(first, second, NT, precision=lax.Precision.HIGHEST)


def shift(value, axis, size, distance):
    return lax.ppermute(value, axis, [(i, (i + distance) % size) for i in range(size)])


def swap(value):
    return lax.ppermute(value, "core", [(0, 1), (1, 0)])


def sum_all(value):
    for axis, size in (("core", NC), ("x", NX), ("rep", NY), ("z", NZ)):
        step = 1
        while step < size:
            value = value + lax.ppermute(value, axis, [(i, i ^ step) for i in range(size)])
            step *= 2
    return value


def tile_order():
    return [
        (half, step, core, spot)
        for half in range(2)
        for step in range(4)
        for core in range(2)
        for spot in range(HALF)
    ]


def tile_number(place, half, step, spot):
    x_at, core_at, y_at = place
    x_owner = lax.rem((y_at if half == 0 else x_at) + step, NX)
    return (x_owner * NZ + half * HALF + spot) * NC + core_at


def build_kernel(place_ref, count_ref, acct_ref, attr_ref, tiles_ref, turned_ref, sums_ref):
    place = place_ref[0], place_ref[1], place_ref[2]
    rows = lax.broadcasted_iota(jnp.int32, (TILE, TILE), 0)
    lanes = lax.broadcasted_iota(jnp.int32, (TILE, TILE), 1)
    for n, (half, step, core, spot) in enumerate(tile_order()):
        t = tile_number(place, half, step, spot)
        account = acct_ref[core, pl.ds(t, 1), :]
        attrib = attr_ref[core, pl.ds(t, 1), :]
        used = lanes < count_ref[core, t]
        account_hot = jnp.where((rows == account) & used, 1.0, 0.0).astype(jnp.bfloat16)
        attrib_hot = jnp.where(rows == attrib, 1.0, 0.0).astype(jnp.bfloat16)
        tile = lax.dot_general(
            account_hot, attrib_hot, NT, preferred_element_type=jnp.float32
        )
        turned = lax.dot_general(
            attrib_hot, account_hot, NT, preferred_element_type=jnp.float32
        )
        tiles_ref[n] = tile.astype(jnp.bfloat16)
        turned_ref[n] = turned.astype(jnp.bfloat16)
        sums_ref[pl.ds(n, 1), :] = jnp.sum(tile, axis=0, keepdims=True)


def build(place, counts, accounts, attribs):
    return pl.pallas_call(
        build_kernel,
        out_shape=(
            shape(64, TILE, TILE, dtype=jnp.bfloat16),
            shape(64, TILE, TILE, dtype=jnp.bfloat16),
            shape(64, TILE),
        ),
        in_specs=[SMEM, SMEM, VMEM, VMEM],
        out_specs=(VMEM, VMEM, VMEM),
        compiler_params=PARAMS,
        name="build_tiles",
    )(place, counts, accounts, attribs)


def pieces(value):
    high = value.astype(jnp.bfloat16)
    rest = value - high.astype(jnp.float32)
    middle = rest.astype(jnp.bfloat16)
    low = (rest - middle.astype(jnp.float32)).astype(jnp.bfloat16)
    return high, middle, low


def gather_kernel(place_ref, home_ref, own_ref, sib_ref, tiles_ref, *refs):
    sums_ref = refs[0] if len(refs) == 10 else None
    outs, split = refs[-9:-1], refs[-1]
    place = place_ref[0], place_ref[1], place_ref[2]
    for core, ref in enumerate((own_ref, sib_ref)):
        for part, piece in enumerate(pieces(ref[...])):
            split[core, part * COLS : (part + 1) * COLS, :] = piece
    for n, (half, step, core, spot) in enumerate(tile_order()):
        home = home_ref[core, tile_number(place, half, step, spot)]
        block = split[core, :, pl.ds(pl.multiple_of(home * TILE, TILE), TILE)]
        parts = jnp.dot(block, tiles_ref[n], preferred_element_type=jnp.float32)
        out = outs[half * 4 + step]
        at = core * HALF + spot
        out[at, :COLS, :] = parts[:COLS] + (parts[COLS : 2 * COLS] + parts[2 * COLS :])
        if sums_ref is not None:
            out[at, COLS:, :] = jnp.broadcast_to(sums_ref[pl.ds(n, 1), :], (8, TILE))


def gather(place, homes, own, sib, tiles, sums):
    rows = COLS if sums is None else COLS + 8
    extra = () if sums is None else (sums,)
    return pl.pallas_call(
        gather_kernel,
        out_shape=tuple(shape(2 * HALF, rows, TILE) for _ in range(8)),
        in_specs=[SMEM, SMEM, VMEM, VMEM, VMEM] + [VMEM] * len(extra),
        out_specs=tuple(VMEM for _ in range(8)),
        scratch_shapes=[pltpu.VMEM((2, 3 * COLS, own.shape[1]), jnp.bfloat16)],
        compiler_params=PARAMS,
        name="gather_tiles",
    )(place, homes, own, sib, tiles, *extra)


def collect_kernel(place_ref, blocks_ref, *refs):
    ins, outs, total = refs[:8], refs[8:16], refs[16]
    for half in range(2):
        mine = place_ref[0] if half == 0 else place_ref[2]
        total[...] = jnp.zeros_like(total)
        for step in range(4):
            for core in range(2):
                for spot in range(HALF):
                    at = core * HALF + spot
                    block = blocks_ref[half * 4 + step, at]
                    slot = lax.rem(block - mine + BLOCKS, BLOCKS)
                    total[slot, spot] += ins[half * 4 + step][at]
        for step in range(4):
            outs[half * 4 + step][...] = total[step]


def collect(place, blocks, arrays):
    rows = arrays[0].shape[1]
    return pl.pallas_call(
        collect_kernel,
        out_shape=tuple(shape(HALF, rows, TILE) for _ in range(8)),
        in_specs=[SMEM, SMEM] + [VMEM] * 8,
        out_specs=tuple(VMEM for _ in range(8)),
        scratch_shapes=[pltpu.VMEM((BLOCKS, HALF, rows, TILE), jnp.float32)],
        compiler_params=PARAMS,
        name="collect_blocks",
    )(place, blocks, *arrays)


def expand_kernel(place_ref, blocks_ref, *refs):
    ins, outs, table = refs[:8], refs[8:16], refs[16]
    for half in range(2):
        mine = place_ref[0] if half == 0 else place_ref[2]
        for step in range(4):
            table[step] = ins[half * 4 + step][...]
        for step in range(4):
            for core in range(2):
                for spot in range(HALF):
                    at = core * HALF + spot
                    block = blocks_ref[half * 4 + step, at]
                    slot = lax.rem(mine - block + BLOCKS, BLOCKS)
                    outs[half * 4 + step][at] = table[slot, spot]


def expand(place, blocks, arrays):
    rows = arrays[0].shape[1]
    return pl.pallas_call(
        expand_kernel,
        out_shape=tuple(shape(2 * HALF, rows, TILE) for _ in range(8)),
        in_specs=[SMEM, SMEM] + [VMEM] * 8,
        out_specs=tuple(VMEM for _ in range(8)),
        scratch_shapes=[pltpu.VMEM((BLOCKS, HALF, rows, TILE), jnp.float32)],
        compiler_params=PARAMS,
        name="expand_blocks",
    )(place, blocks, *arrays)


def spread_kernel(place_ref, home_ref, turned_ref, *refs):
    ins, outs = refs[:8], refs[8:10]
    place = place_ref[0], place_ref[1], place_ref[2]
    for out in outs:
        out[...] = jnp.zeros_like(out)
    rows = outs[0].shape[0]
    for n, (half, step, core, spot) in enumerate(tile_order()):
        home = home_ref[core, tile_number(place, half, step, spot)]
        value = ins[half * 4 + step][core * HALF + spot]
        stack = jnp.concatenate([p.astype(jnp.float32) for p in pieces(value)], axis=0)
        parts = jnp.dot(
            stack.astype(jnp.bfloat16), turned_ref[n], preferred_element_type=jnp.float32
        )
        where = pl.ds(pl.multiple_of(home * TILE, TILE), TILE)
        outs[core][:, where] += parts[:rows] + (parts[rows : 2 * rows] + parts[2 * rows :])


def spread(place, homes, turned, arrays, accounts):
    rows = arrays[0].shape[1]
    return pl.pallas_call(
        spread_kernel,
        out_shape=(shape(rows, accounts), shape(rows, accounts)),
        in_specs=[SMEM, SMEM, VMEM] + [VMEM] * 8,
        out_specs=(VMEM, VMEM),
        compiler_params=PARAMS,
        name="spread_tiles",
    )(place, homes, turned, *arrays)


def send_halves(arrays, near, far, sign):
    got = []
    for half, axis in ((0, near), (1, far)):
        size = NY if axis == "rep" else NX
        got.append(arrays[half * 4])
        for step in range(1, 4):
            got.append(shift(arrays[half * 4 + step], axis, size, sign * step))
    return got


def couple(place, homes, blocks, tiles, turned, weight, own, sib, sums):
    messages = gather(place, homes, own, sib, tiles, sums)
    arrived = send_halves(messages, "rep", "x", 1)
    dense = collect(place, blocks, arrived)
    arrived = send_halves(dense, "x", "rep", 1)
    halves = [
        (arrived[h] + arrived[h + 1]) + (arrived[h + 2] + arrived[h + 3]) for h in (0, 4)
    ]
    parts = lax.all_to_all(
        jnp.concatenate(halves, axis=0), "z", split_axis=0, concat_axis=0, tiled=True
    )
    scaled = jnp.sum(parts, axis=0) * weight
    values = lax.all_to_all(
        jnp.broadcast_to(scaled, parts.shape), "z", split_axis=0, concat_axis=0, tiled=True
    )
    arrived = send_halves(
        [values[:HALF]] * 4 + [values[HALF:]] * 4, "x", "rep", 1
    )
    entries = expand(place, blocks, arrived)
    arrived = send_halves(entries, "rep", "x", -1)
    mine, other = spread(place, homes, turned, arrived, own.shape[1])
    return mine + swap(other)


def shards(
    right_side, tile_account, tile_attribute, tile_count, tile_home, tile_block, attribute_weight
):
    x_at, z_at = lax.axis_index("x"), lax.axis_index("z")
    core_at, y_at = lax.axis_index("core"), lax.axis_index("rep")
    place = jnp.stack([x_at, core_at, y_at])
    start = right_side.T

    info = jnp.concatenate(
        [
            tile_account,
            tile_attribute,
            jnp.pad(jnp.stack([tile_count, tile_home, tile_block]), ((0, 5), (0, 64))),
        ],
        axis=0,
    )
    info = jnp.stack([info, swap(info)])
    accounts, attribs = info[:, :64], info[:, 64:128]
    counts, homes, tile_blocks = info[:, 128, :64], info[:, 129, :64], info[:, 130, :64]
    by_owner = lax.dynamic_index_in_dim(
        tile_blocks.reshape(2, NX, 2, HALF, NC), core_at, 4, keepdims=False
    )
    blocks = []
    for half, axis, at in ((0, "rep", y_at), (1, "x", x_at)):
        for step in range(4):
            ids = lax.dynamic_index_in_dim(
                by_owner[:, :, half], lax.rem(at + step, NX), 1, keepdims=False
            ).reshape(2 * HALF)
            blocks.append(ids if step == 0 else shift(ids, axis, 4, step))
    blocks = jnp.stack(blocks)

    own_weight = attribute_weight.reshape(BLOCKS, TILE)
    all_weight = lax.all_gather(own_weight, "x", axis=0, tiled=False)
    first = lax.dynamic_index_in_dim(
        lax.dynamic_index_in_dim(all_weight, y_at, 0, keepdims=False), x_at, 0, keepdims=False
    )
    second = lax.dynamic_index_in_dim(own_weight, y_at, 0, keepdims=False)
    weight = jnp.where(z_at < HALF, first, second).astype(jnp.float32)[None, :]

    tiles, turned, sums = build(place, counts, accounts, attribs)

    def link(vector, with_sums):
        return couple(
            place,
            homes,
            blocks,
            tiles,
            turned,
            weight,
            vector,
            swap(vector),
            sums if with_sums else None,
        )

    linked = link(start, True)
    degree = linked[COLS : COLS + 1]
    product = start + COUPLING * (degree * start - linked[:COLS])

    def operate(vector):
        return vector + COUPLING * (degree * vector - link(vector, False))

    grams = sum_all(
        jnp.concatenate([gram(start, start), gram(start, product), gram(product, product)])
    )
    res_gram, curvature, square = grams[:COLS], grams[COLS : 2 * COLS], grams[2 * COLS :]
    step_0 = solve_spd(curvature, res_gram)
    cross = mul(curvature, step_0)
    next_gram = res_gram - cross - cross.T + mul(step_0.T, mul(square, step_0))
    update_0 = solve_spd(res_gram, next_gram)
    twice = operate(product)

    residual = start - mul(step_0.T, product)
    direction = residual + mul(update_0.T, start)
    image = product - mul(step_0.T, twice)
    product_1 = image + mul(update_0.T, product)

    grams = sum_all(
        jnp.concatenate(
            [
                gram(residual, residual),
                gram(direction, product_1),
                gram(residual, product_1),
                gram(product_1, product_1),
            ]
        )
    )
    res_gram, curvature, mixed, square = (grams[i * COLS : (i + 1) * COLS] for i in range(4))
    step_1 = solve_spd(curvature, res_gram)
    cross = mul(mixed, step_1)
    next_gram = res_gram - cross - cross.T + mul(step_1.T, mul(square, step_1))
    update_1 = solve_spd(res_gram, next_gram)
    twice = operate(product_1)

    solution_2 = mul(step_0.T, start) + mul(step_1.T, direction)
    residual = residual - mul(step_1.T, product_1)
    direction = residual + mul(update_1.T, direction)
    product_2 = image - mul(step_1.T, twice) + mul(update_1.T, product_1)

    grams = sum_all(
        jnp.concatenate([gram(residual, residual), gram(direction, product_2)])
    )
    step_2 = solve_spd(grams[COLS:], grams[:COLS])
    answer = solution_2 + mul(step_2.T, direction)
    residual = residual - mul(step_2.T, product_2)
    return (answer.T, residual.T)


def solution(mesh):
    fine = Mesh(mesh.devices.reshape(NX, NZ, NC, NY), ALL)
    rows, flat = P(ALL, None), P(ALL)
    return jax.shard_map(
        shards,
        mesh=fine,
        in_specs=(rows, rows, rows, flat, flat, flat, P(("x", "z", "core"))),
        out_specs=(rows, rows),
        check_vma=False,
    )
```

time: 1080 us -> 512 us (0.47)
  blocking collectives: 495 us -> 27.3 us
  waiting for transfers between devices: 288 us -> 168 us
  starting transfers between devices: 71.9 us -> 150 us
  matrix products: 112 us -> 37 us
  Pallas kernels: 0 us -> 26.8 us
  between operations: 14.5 us -> 2.07 us
    psum x6 -> x0, blocking collectives: 382 us -> none  [the longest x2 151 us: shards(): curvature = lax.psum(inner_gram(direction, product), ('acct', 'rep'))]
    ppermute x0 -> x109, waiting for transfers between devices: none -> 151 us  [the longest x24 82.3 us: sum_all(): lax.ppermute(value, axis, [(i, i ^ step) for i in range(size)])]
    all_to_all x7 -> x5, waiting for transfers between devices: 167 us -> 16.9 us  [the longest x2 8.95 us: couple(): lax.all_to_all(jnp.broadcast_to(scaled, parts.shape), 'z', split_axis=0,...]
    ppermute x0 -> x109, starting transfers between devices: none -> 127 us  [the longest x78 106 us: shift(): lax.ppermute(value, axis, [(i, (i + distance) % size) for i in range(size)])]
    psum x3 -> x0, waiting for transfers between devices: 122 us -> none  [shards(): summed = lax.psum(summed, 'rep')]
    all_to_all x2 -> x1, blocking collectives: 113 us -> 17.1 us  [couple(): lax.all_to_all(jnp.broadcast_to(scaled, parts.shape), 'z', split_axis=0,...]
    dot_general x34 -> x27, matrix products: 110 us -> 33.4 us  [the longest x18 24.5 us: mul(): return jnp.dot(first, second, precision=lax.Precision.HIGHEST)]
    all_to_all x7 -> x5, starting transfers between devices: 71.6 us -> 22.9 us  [the longest x3 15.9 us: couple(): lax.all_to_all(jnp.concatenate(halves, axis=0), 'z', split_axis=0, concat...]
  transfers between devices with their start and end apart: 10 -> 114, of which waited for: 8 -> 61; matrix products, arithmetic and copies ran while one was open for 4% -> 17% of each run, Pallas kernels for 0% -> 2%
where the time goes in v1:
time: 512 us; the launch traced here: 504 us
  waiting for transfers between devices  168 us (33%)
  starting transfers between devices  150 us (29%)
  other arithmetic  69.7 us (14%)
  matrix products  37 us (7%)
  blocking collectives  27.3 us (5%)
  Pallas kernels  26.8 us (5%)
  local copies, waits for them, and re-layouts  23 us (4%)
    ppermute x78, starting transfers between devices, shift(): lax.ppermute(value, axis, [(i, (i + distance) % size) for i in range(size)])  106 us
    ppermute x24, waiting for transfers between devices, sum_all(): lax.ppermute(value, axis, [(i, i ^ step) for i in range(size)])  82.3 us
    ppermute x78, waiting for transfers between devices, shift(): lax.ppermute(value, axis, [(i, (i + distance) % size) for i in range(size)])  64.6 us
    another operation x15, other arithmetic, solve_spd(): factor = jnp.linalg.cholesky(matrix)  32.7 us
    another operation x10, other arithmetic, solve_spd(): lax.linalg.triangular_solve(factor, partway, left_side=True, lower=True,...  31.7 us
    dot_general x18, matrix products, mul(): return jnp.dot(first, second, precision=lax.Precision.HIGHEST)  24.5 us
    ppermute x24, starting transfers between devices, sum_all(): lax.ppermute(value, axis, [(i, i ^ step) for i in range(size)])  19.9 us
    unnamed x88, local copies, waits for them, and re-layouts  17.4 us
  transfers between devices with their start and end apart: 114, of which 61 were waited for; matrix products, arithmetic and copies ran while one was open for 17% of the time, Pallas kernels for 2%

profile of v1, /device:TPU:26, one launch (start us, length us, event | category | flops | bytes accessed | tf_op | source)
XLA Modules:
  0.0 503.7 jit_solution(8429503312222087976)
XLA Ops:
  36.9 3.9 collective-permute-done.10.refs_3_
  62.5 8.9 %all-to-all-start = ((f32[8,72,128]{2,1,0:T(8,128)}), f32[8,72,128]{2,1,0:T(8,128)S(1)}, u32[]{:S(2)}, u32[]{:S(2)}) async-start(f32[8,72,128]{2,1,0:T(8,128)} %pad_maximum_fusion), calls=%async_computation | async-start | bytes 589824 | tf_op jit(solution)/shard_map/all_to_all | solution.py:256
  71.4 10.1 %all_gather.3 = s32[4,4,128]{2,1,0:T(4,128)S(1)} all-gather(s32[1,4,128]{2,1,0:T(4,128)S(1)} %bitcast.181), channel_id=1, replica_groups=mesh['x'=4,'z'=8,'core'=2,'rep'=4] {'x'}, dimensions={0}, use_global_device_ids=true | all-gather | bytes 10240 | tf_op jit(solution)/shard_map/all_gather | solution.py:304
  82.3 17.1 %all_to_all.30 = f32[8,72,128]{2,1,0:T(8,128)S(1)} all-to-all(f32[8,72,128]{2,1,0:T(8,128)S(1)} %broadcast_in_dim.11), channel_id=1, replica_groups=mesh['x'=4,'z'=8,'core'=2,'rep'=4] {'z'}, dimensions={0} | all-to-all | bytes 589824 | tf_op jit(solution)/shard_map/all_to_all | solution.py:260
  118.5 3.8 collective-permute-start.29
  126.5 4.0 collective-permute-done.30.refs_6_
  130.5 4.3 collective-permute-done.31.refs_7_
  147.6 3.7 collective-permute-start.34
  154.2 5.7 %collective-permute-done.35 = f32[192,64]{0,1:T(8,128)S(1)} collective-permute-done((f32[192,64]{0,1:T(8,128)S(1)}, f32[192,64]{0,1:T(8,128)S(1)}, u32[]{:S(2)}, u32[]{:S(2)}) %collective-permute-start.35) | collective-permute-done | bytes 49184 | tf_op jit(solution)/shard_map/ppermute | solution.py:54
  188.9 6.0 %collective-permute-done.39 = f32[192,64]{0,1:T(8,128)S(1)} collective-permute-done((f32[192,64]{0,1:T(8,128)S(1)}, f32[192,64]{0,1:T(8,128)S(1)}, u32[]{:S(2)}, u32[]{:S(2)}) %collective-permute-start.39) | collective-permute-done | bytes 49184 | tf_op jit(solution)/shard_map/ppermute | solution.py:54
  196.1 7.6 %collective-permute-done.40 = f32[192,64]{0,1:T(8,128)S(1)} collective-permute-done((f32[192,64]{0,1:T(8,128)S(1)}, f32[192,64]{0,1:T(8,128)S(1)}, u32[]{:S(2)}, u32[]{:S(2)}) %collective-permute-start.40) | collective-permute-done | bytes 49184 | tf_op jit(solution)/shard_map/ppermute | solution.py:54
  217.6 5.9 %cholesky.89 = f32[64,64]{1,0:T(8,128)S(1)} custom-call(f32[64,64]{1,0:T(8,128)S(1)} %get-tuple-element.193), custom_call_target="Cholesky" | custom-call | tf_op jit(solution)/shard_map/jit(cholesky)/cholesky | solution.py:27
  232.7 4.9 custom-call.17
  238.0 4.5 all-to-all-done.3
  251.4 5.8 %cholesky.100 = f32[64,64]{1,0:T(8,128)S(1)} custom-call(f32[64,64]{1,0:T(8,128)S(1)} %get-tuple-element.192), custom_call_target="Cholesky" | custom-call | tf_op jit(solution)/shard_map/jit(cholesky)/cholesky | solution.py:27
  276.7 6.3 %custom-call.19 = f32[1,64,64]{1,2,0:T(8,128)} custom-call(f32[1,64,64]{2,1,0:T(8,128)} %fusion.21), custom_call_target="InvertDiagBlocksLowerTriangular" | custom-call | tf_op jit(solution)/shard_map/triangular_solve/custom-call.2 | solution.py:29
  300.7 4.3 collective-permute-done.68
  311.1 6.5 %collective-permute-done.70 = f32[256,64]{0,1:T(8,128)S(1)} collective-permute-done((f32[256,64]{0,1:T(8,128)S(1)}, f32[256,64]{0,1:T(8,128)S(1)}, u32[]{:S(2)}, u32[]{:S(2)}) %collective-permute-start.70) | collective-permute-done | bytes 65568 | tf_op jit(solution)/shard_map/ppermute | solution.py:54
  318.6 4.8 collective-permute-done.71
  346.8 7.1 %collective-permute-done.74 = f32[256,64]{0,1:T(8,128)S(1)} collective-permute-done((f32[256,64]{0,1:T(8,128)S(1)}, f32[256,64]{0,1:T(8,128)S(1)}, u32[]{:S(2)}, u32[]{:S(2)}) %collective-permute-start.74) | collective-permute-done | bytes 65568 | tf_op jit(solution)/shard_map/ppermute | solution.py:54
  368.1 5.9 %cholesky.111 = f32[64,64]{1,0:T(8,128)S(1)} custom-call(f32[64,64]{1,0:T(8,128)S(1)} %get-tuple-element.189), custom_call_target="Cholesky" | custom-call | tf_op jit(solution)/shard_map/jit(cholesky)/cholesky | solution.py:27
  383.3 4.9 custom-call.21
  388.6 4.5 all-to-all-done.5
  402.5 5.8 %cholesky.122 = f32[64,64]{1,0:T(8,128)S(1)} custom-call(f32[64,64]{1,0:T(8,128)S(1)} %get-tuple-element.188), custom_call_target="Cholesky" | custom-call | tf_op jit(solution)/shard_map/jit(cholesky)/cholesky | solution.py:27
  427.5 6.3 %custom-call.23 = f32[1,64,64]{1,2,0:T(8,128)} custom-call(f32[1,64,64]{2,1,0:T(8,128)} %fusion.23), custom_call_target="InvertDiagBlocksLowerTriangular" | custom-call | tf_op jit(solution)/shard_map/triangular_solve/custom-call.2 | solution.py:29
  454.7 3.7 collective-permute-done.103
  458.5 3.9 collective-permute-done.104
  463.6 4.2 collective-permute-done.105
  472.9 4.3 collective-permute-done.107
  480.9 4.2 collective-permute-done.108
  485.4 5.9 %cholesky.133 = f32[64,64]{1,0:T(8,128)S(1)} custom-call(f32[64,64]{1,0:T(8,128)S(1)} %fusion.36), custom_call_target="Cholesky" | custom-call | tf_op jit(solution)/shard_map/jit(cholesky)/cholesky | solution.py:27
  492.6 4.9 custom-call.25
  (444 shorter events, 318.0 us)
Async XLA Ops:
  15.0 16.7 %collective-permute-start.8 = (f32[8,72,128]{2,1,0:T(8,128)}, f32[8,72,128]{2,1,0:T(8,128)S(1)}, u32[]{:S(2)}, u32[]{:S(2)}) collective-permute-start(f32[8,72,128]{2,1,0:T(8,128)} %get-tuple-element.90), channel_id=1, source_target_pairs={{0,1},{1,2},{2,3},{3,0},{4,5},{5,6},{6,7},{7,4},{8,9},{9,10},{10,1... | collective-permute-start | bytes 884744 | tf_op jit(solution)/shard_map/ppermute | solution.py:43
  27.3 13.4 %collective-permute-start.10 = (f32[8,72,128]{2,1,0:T(8,128)}, f32[8,72,128]{2,1,0:T(8,128)S(1)}, u32[]{:S(2)}, u32[]{:S(2)}) collective-permute-start(f32[8,72,128]{2,1,0:T(8,128)} %copy-done.21), channel_id=1, source_target_pairs={{0,3},{1,0},{2,1},{3,2},{4,7},{5,4},{6,5},{7,6},{8,11},{9,8},{10,9... | collective-permute-start | bytes 884744 | tf_op jit(solution)/shard_map/ppermute | solution.py:43
  31.8 12.7 %collective-permute-start.13 = (f32[8,72,128]{2,1,0:T(8,128)}, f32[8,72,128]{2,1,0:T(8,128)}, u32[]{:S(2)}, u32[]{:S(2)}) collective-permute-start(f32[8,72,128]{2,1,0:T(8,128)} %copy-done.18), channel_id=1, source_target_pairs={{0,192},{64,0},{128,64},{192,128},{1,193},{65,1},{129,65},{193,129... | collective-permute-start | bytes 884744 | tf_op jit(solution)/shard_map/ppermute | solution.py:43
  62.5 19.8 %all-to-all-start = ((f32[8,72,128]{2,1,0:T(8,128)}), f32[8,72,128]{2,1,0:T(8,128)S(1)}, u32[]{:S(2)}, u32[]{:S(2)}) async-start(f32[8,72,128]{2,1,0:T(8,128)} %pad_maximum_fusion), calls=%async_computation | async-start | bytes 589824 | tf_op jit(solution)/shard_map/all_to_all | solution.py:256
  113.7 12.3 %collective-permute-start.27 = (f32[8,72,128]{2,1,0:T(8,128)S(1)}, f32[8,72,128]{2,1,0:T(8,128)S(1)}, u32[]{:S(2)}, u32[]{:S(2)}) collective-permute-start(f32[8,72,128]{2,1,0:T(8,128)S(1)} %get-tuple-element.107), channel_id=1, source_target_pairs={{0,2},{1,3},{2,0},{3,1},{4,6},{5,7},{6,4},{7,5},{8,10},{9,11},{10,... | collective-permute-start | bytes 884744 | tf_op jit(solution)/shard_map/ppermute | solution.py:43
  147.4 26.1 %collective-permute-start.42 = (f32[8,64,128]{2,1,0:T(8,128)S(1)}, f32[8,64,128]{2,1,0:T(8,128)S(1)}, u32[]{:S(2)}, u32[]{:S(2)}) collective-permute-start(f32[8,64,128]{2,1,0:T(8,128)S(1)} %get-tuple-element.116), channel_id=1, source_target_pairs={{0,1},{1,2},{2,3},{3,0},{4,5},{5,6},{6,7},{7,4},{8,9},{9,10},{10,1... | collective-permute-start | bytes 786440 | tf_op jit(solution)/shard_map/ppermute | solution.py:43
  175.8 12.5 %collective-permute-start.38 = (f32[192,64]{0,1:T(8,128)S(1)}, f32[192,64]{0,1:T(8,128)S(1)}, u32[]{:S(2)}, u32[]{:S(2)}) collective-permute-start(f32[192,64]{0,1:T(8,128)S(1)} %add.269), channel_id=1, source_target_pairs={{0,8},{8,0},{16,24},{24,16},{32,40},{40,32},{48,56},{56,48},{1,9},... | collective-permute-start | bytes 147464 | tf_op jit(solution)/shard_map/ppermute | solution.py:54
  182.9 22.8 %collective-permute-start.48 = (f32[4,64,128]{2,1,0:T(8,128)S(1)}, f32[4,64,128]{2,1,0:T(8,128)S(1)}, u32[]{:S(2)}, u32[]{:S(2)}) collective-permute-start(f32[4,64,128]{2,1,0:T(8,128)S(1)} %get-tuple-element.124), channel_id=1, source_target_pairs={{0,64},{64,128},{128,192},{192,0},{1,65},{65,129},{129,193},{193,1... | collective-permute-start | bytes 393224 | tf_op jit(solution)/shard_map/ppermute | solution.py:43
  183.6 22.4 %collective-permute-start.49 = (f32[4,64,128]{2,1,0:T(8,128)S(1)}, f32[4,64,128]{2,1,0:T(8,128)S(1)}, u32[]{:S(2)}, u32[]{:S(2)}) collective-permute-start(f32[4,64,128]{2,1,0:T(8,128)S(1)} %get-tuple-element.125), channel_id=1, source_target_pairs={{0,128},{64,192},{128,0},{192,64},{1,129},{65,193},{129,1},{193,65... | collective-permute-start | bytes 393224 | tf_op jit(solution)/shard_map/ppermute | solution.py:43
  186.3 19.7 %collective-permute-start.50 = (f32[4,64,128]{2,1,0:T(8,128)S(1)}, f32[4,64,128]{2,1,0:T(8,128)S(1)}, u32[]{:S(2)}, u32[]{:S(2)}) collective-permute-start(f32[4,64,128]{2,1,0:T(8,128)S(1)} %get-tuple-element.126), channel_id=1, source_target_pairs={{0,192},{64,0},{128,64},{192,128},{1,193},{65,1},{129,65},{193,129... | collective-permute-start | bytes 393224 | tf_op jit(solution)/shard_map/ppermute | solution.py:43
  213.7 14.2 %all-to-all-start.2 = ((f32[8,64,128]{2,1,0:T(8,128)}), f32[8,64,128]{2,1,0:T(8,128)S(1)}, u32[]{:S(2)}, u32[]{:S(2)}) async-start(f32[8,64,128]{2,1,0:T(8,128)} %pad_maximum_fusion.1), calls=%async_computation.2 | async-start | bytes 524288 | tf_op jit(solution)/shard_map/all_to_all | solution.py:256
  228.6 13.9 %all-to-all-start.3 = ((f32[8,64,128]{2,1,0:T(8,128)}), f32[8,64,128]{2,1,0:T(8,128)S(1)}, u32[]{:S(2)}, u32[]{:S(2)}) async-start(f32[8,64,128]{2,1,0:T(8,128)} %broadcast_in_dim.12), calls=%async_computation.3 | async-start | bytes 524288 | tf_op jit(solution)/shard_map/all_to_all | solution.py:260
  243.0 14.3 %collective-permute-start.58 = (f32[4,64,128]{2,1,0:T(8,128)S(1)}, f32[4,64,128]{2,1,0:T(8,128)S(1)}, u32[]{:S(2)}, u32[]{:S(2)}) collective-permute-start(f32[4,64,128]{2,1,0:T(8,128)S(1)} %get-tuple-element.179.refs_4_), channel_id=1, source_target_pairs={{0,2},{1,3},{2,0},{3,1},{4,6},{5,7},{6,4},{7,5},{8,10},{9,11},{10,... | collective-permute-start | bytes 393224 | tf_op jit(solution)/shard_map/ppermute | solution.py:43
  245.1 12.2 %collective-permute-start.57 = (f32[4,64,128]{2,1,0:T(8,128)S(1)}, f32[4,64,128]{2,1,0:T(8,128)S(1)}, u32[]{:S(2)}, u32[]{:S(2)}) collective-permute-start(f32[4,64,128]{2,1,0:T(8,128)S(1)} %get-tuple-element.179.refs_4_), channel_id=1, source_target_pairs={{0,1},{1,2},{2,3},{3,0},{4,5},{5,6},{6,7},{7,4},{8,9},{9,10},{10,1... | collective-permute-start | bytes 393224 | tf_op jit(solution)/shard_map/ppermute | solution.py:43
  265.0 19.7 %collective-permute-start.61 = (f32[8,64,128]{2,1,0:T(8,128)}, f32[8,64,128]{2,1,0:T(8,128)S(1)}, u32[]{:S(2)}, u32[]{:S(2)}) collective-permute-start(f32[8,64,128]{2,1,0:T(8,128)} %get-tuple-element.133), channel_id=1, source_target_pairs={{0,2},{1,3},{2,0},{3,1},{4,6},{5,7},{6,4},{7,5},{8,10},{9,11},{10,... | collective-permute-start | bytes 786440 | tf_op jit(solution)/shard_map/ppermute | solution.py:43
  266.0 18.7 %collective-permute-start.62 = (f32[8,64,128]{2,1,0:T(8,128)}, f32[8,64,128]{2,1,0:T(8,128)S(1)}, u32[]{:S(2)}, u32[]{:S(2)}) collective-permute-start(f32[8,64,128]{2,1,0:T(8,128)} %get-tuple-element.134), channel_id=1, source_target_pairs={{0,1},{1,2},{2,3},{3,0},{4,5},{5,6},{6,7},{7,4},{8,9},{9,10},{10,1... | collective-permute-start | bytes 786440 | tf_op jit(solution)/shard_map/ppermute | solution.py:43
  268.3 16.4 %collective-permute-start.63 = (f32[8,64,128]{2,1,0:T(8,128)}, f32[8,64,128]{2,1,0:T(8,128)}, u32[]{:S(2)}, u32[]{:S(2)}) collective-permute-start(f32[8,64,128]{2,1,0:T(8,128)} %get-tuple-element.136), channel_id=1, source_target_pairs={{0,192},{64,0},{128,64},{192,128},{1,193},{65,1},{129,65},{193,129... | collective-permute-start | bytes 786440 | tf_op jit(solution)/shard_map/ppermute | solution.py:43
  270.4 14.4 %collective-permute-start.64 = (f32[8,64,128]{2,1,0:T(8,128)}, f32[8,64,128]{2,1,0:T(8,128)}, u32[]{:S(2)}, u32[]{:S(2)}) collective-permute-start(f32[8,64,128]{2,1,0:T(8,128)} %get-tuple-element.137), channel_id=1, source_target_pairs={{0,128},{64,192},{128,0},{192,64},{1,129},{65,193},{129,1},{193,65... | collective-permute-start | bytes 786440 | tf_op jit(solution)/shard_map/ppermute | solution.py:43
  272.4 12.3 %collective-permute-start.65 = (f32[8,64,128]{2,1,0:T(8,128)}, f32[8,64,128]{2,1,0:T(8,128)}, u32[]{:S(2)}, u32[]{:S(2)}) collective-permute-start(f32[8,64,128]{2,1,0:T(8,128)} %get-tuple-element.138), channel_id=1, source_target_pairs={{0,64},{64,128},{128,192},{192,0},{1,65},{65,129},{129,193},{193,1... | collective-permute-start | bytes 786440 | tf_op jit(solution)/shard_map/ppermute | solution.py:43
  308.4 22.3 %collective-permute-start.76 = (f32[8,64,128]{2,1,0:T(8,128)S(1)}, f32[8,64,128]{2,1,0:T(8,128)S(1)}, u32[]{:S(2)}, u32[]{:S(2)}) collective-permute-start(f32[8,64,128]{2,1,0:T(8,128)S(1)} %get-tuple-element.142), channel_id=1, source_target_pairs={{0,1},{1,2},{2,3},{3,0},{4,5},{5,6},{6,7},{7,4},{8,9},{9,10},{10,1... | collective-permute-start | bytes 786440 | tf_op jit(solution)/shard_map/ppermute | solution.py:43
  332.4 12.9 %collective-permute-start.73 = (f32[256,64]{0,1:T(8,128)S(1)}, f32[256,64]{0,1:T(8,128)S(1)}, u32[]{:S(2)}, u32[]{:S(2)}) collective-permute-start(f32[256,64]{0,1:T(8,128)S(1)} %add.289), channel_id=1, source_target_pairs={{0,16},{8,24},{16,0},{24,8},{32,48},{40,56},{48,32},{56,40},{1,17}... | collective-permute-start | bytes 196616 | tf_op jit(solution)/shard_map/ppermute | solution.py:54
  339.6 17.4 %collective-permute-start.82 = (f32[4,64,128]{2,1,0:T(8,128)S(1)}, f32[4,64,128]{2,1,0:T(8,128)S(1)}, u32[]{:S(2)}, u32[]{:S(2)}) collective-permute-start(f32[4,64,128]{2,1,0:T(8,128)S(1)} %get-tuple-element.150), channel_id=1, source_target_pairs={{0,64},{64,128},{128,192},{192,0},{1,65},{65,129},{129,193},{193,1... | collective-permute-start | bytes 393224 | tf_op jit(solution)/shard_map/ppermute | solution.py:43
  340.2 16.7 %collective-permute-start.83 = (f32[4,64,128]{2,1,0:T(8,128)S(1)}, f32[4,64,128]{2,1,0:T(8,128)S(1)}, u32[]{:S(2)}, u32[]{:S(2)}) collective-permute-start(f32[4,64,128]{2,1,0:T(8,128)S(1)} %get-tuple-element.151), channel_id=1, source_target_pairs={{0,128},{64,192},{128,0},{192,64},{1,129},{65,193},{129,1},{193,65... | collective-permute-start | bytes 393224 | tf_op jit(solution)/shard_map/ppermute | solution.py:43
  343.3 13.7 %collective-permute-start.84 = (f32[4,64,128]{2,1,0:T(8,128)S(1)}, f32[4,64,128]{2,1,0:T(8,128)S(1)}, u32[]{:S(2)}, u32[]{:S(2)}) collective-permute-start(f32[4,64,128]{2,1,0:T(8,128)S(1)} %get-tuple-element.152), channel_id=1, source_target_pairs={{0,192},{64,0},{128,64},{192,128},{1,193},{65,1},{129,65},{193,129... | collective-permute-start | bytes 393224 | tf_op jit(solution)/shard_map/ppermute | solution.py:43
  364.4 13.9 %all-to-all-start.4 = ((f32[8,64,128]{2,1,0:T(8,128)}), f32[8,64,128]{2,1,0:T(8,128)S(1)}, u32[]{:S(2)}, u32[]{:S(2)}) async-start(f32[8,64,128]{2,1,0:T(8,128)} %pad_maximum_fusion.2), calls=%async_computation.4 | async-start | bytes 524288 | tf_op jit(solution)/shard_map/all_to_all | solution.py:256
  379.0 14.0 %all-to-all-start.5 = ((f32[8,64,128]{2,1,0:T(8,128)}), f32[8,64,128]{2,1,0:T(8,128)S(1)}, u32[]{:S(2)}, u32[]{:S(2)}) async-start(f32[8,64,128]{2,1,0:T(8,128)} %broadcast_in_dim.13), calls=%async_computation.5 | async-start | bytes 524288 | tf_op jit(solution)/shard_map/all_to_all | solution.py:260
  394.0 14.4 %collective-permute-start.92 = (f32[4,64,128]{2,1,0:T(8,128)S(1)}, f32[4,64,128]{2,1,0:T(8,128)S(1)}, u32[]{:S(2)}, u32[]{:S(2)}) collective-permute-start(f32[4,64,128]{2,1,0:T(8,128)S(1)} %get-tuple-element.177.refs_4_), channel_id=1, source_target_pairs={{0,2},{1,3},{2,0},{3,1},{4,6},{5,7},{6,4},{7,5},{8,10},{9,11},{10,... | collective-permute-start | bytes 393224 | tf_op jit(solution)/shard_map/ppermute | solution.py:43
  396.1 12.3 %collective-permute-start.91 = (f32[4,64,128]{2,1,0:T(8,128)S(1)}, f32[4,64,128]{2,1,0:T(8,128)S(1)}, u32[]{:S(2)}, u32[]{:S(2)}) collective-permute-start(f32[4,64,128]{2,1,0:T(8,128)S(1)} %get-tuple-element.177.refs_4_), channel_id=1, source_target_pairs={{0,1},{1,2},{2,3},{3,0},{4,5},{5,6},{6,7},{7,4},{8,9},{9,10},{10,1... | collective-permute-start | bytes 393224 | tf_op jit(solution)/shard_map/ppermute | solution.py:43
  417.0 19.3 %collective-permute-start.95 = (f32[8,64,128]{2,1,0:T(8,128)}, f32[8,64,128]{2,1,0:T(8,128)S(1)}, u32[]{:S(2)}, u32[]{:S(2)}) collective-permute-start(f32[8,64,128]{2,1,0:T(8,128)} %get-tuple-element.159), channel_id=1, source_target_pairs={{0,2},{1,3},{2,0},{3,1},{4,6},{5,7},{6,4},{7,5},{8,10},{9,11},{10,... | collective-permute-start | bytes 786440 | tf_op jit(solution)/shard_map/ppermute | solution.py:43
  419.1 17.3 %collective-permute-start.96 = (f32[8,64,128]{2,1,0:T(8,128)}, f32[8,64,128]{2,1,0:T(8,128)S(1)}, u32[]{:S(2)}, u32[]{:S(2)}) collective-permute-start(f32[8,64,128]{2,1,0:T(8,128)} %get-tuple-element.160), channel_id=1, source_target_pairs={{0,1},{1,2},{2,3},{3,0},{4,5},{5,6},{6,7},{7,4},{8,9},{9,10},{10,1... | collective-permute-start | bytes 786440 | tf_op jit(solution)/shard_map/ppermute | solution.py:43
  421.8 14.5 %collective-permute-start.97 = (f32[8,64,128]{2,1,0:T(8,128)}, f32[8,64,128]{2,1,0:T(8,128)}, u32[]{:S(2)}, u32[]{:S(2)}) collective-permute-start(f32[8,64,128]{2,1,0:T(8,128)} %get-tuple-element.162), channel_id=1, source_target_pairs={{0,192},{64,0},{128,64},{192,128},{1,193},{65,1},{129,65},{193,129... | collective-permute-start | bytes 786440 | tf_op jit(solution)/shard_map/ppermute | solution.py:43
  421.8 14.5 %collective-permute-start.98 = (f32[8,64,128]{2,1,0:T(8,128)}, f32[8,64,128]{2,1,0:T(8,128)}, u32[]{:S(2)}, u32[]{:S(2)}) collective-permute-start(f32[8,64,128]{2,1,0:T(8,128)} %get-tuple-element.163), channel_id=1, source_target_pairs={{0,128},{64,192},{128,0},{192,64},{1,129},{65,193},{129,1},{193,65... | collective-permute-start | bytes 786440 | tf_op jit(solution)/shard_map/ppermute | solution.py:43
  (126 other events, 848.1 us)
